TPU v7x, 32 devices: a whole 2x2x4 slice. The times are simulated.
32 devices in a mesh: batch: 4 (over y, x), wide: 8 (over z, core).
Axes of the slice: x: 2, y: 2, z: 4, core: 2. Of those that a mesh axis runs over, the one named last changes fastest.
Arguments:
- inputs: bfloat16 [64, 1024, 256], P('batch', 'wide'), may hold values from -6 to 6
- lengths: int32 [64], P('batch'), may hold values from 256 to 1024, as said below
- ln1_gain: float32 [2, 256], replicated, may hold values from 0.5 to 1.5
- ln1_bias: float32 [2, 256], replicated, may hold values from -1.5 to 1.5
- w_qkv: bfloat16 [2, 256, 768], replicated, may hold values from -0.5 to 0.5
- w_out: bfloat16 [2, 256, 256], replicated, may hold values from -1.5 to 1.5
- ln2_gain: float32 [2, 256], replicated, may hold values from 0.5 to 1.5
- ln2_bias: float32 [2, 256], replicated, may hold values from -1.5 to 1.5
- w_up: bfloat16 [2, 256, 1024], replicated, may hold values from -0.375 to 0.375
- w_down: bfloat16 [2, 1024, 256], replicated, may hold values from -0.25 to 0.25
- cotangent: bfloat16 [64, 1024, 256], P('batch', 'wide'), may hold values from -6 to 6
Outputs:
- outputs: bfloat16 [64, 1024, 256], P('batch', 'wide')
- grad_inputs: float32 [64, 1024, 256], P('batch', 'wide')
- grad_ln1_gain: float32 [2, 256], replicated
- grad_ln1_bias: float32 [2, 256], replicated
- grad_w_qkv: float32 [2, 256, 768], replicated
- grad_w_out: float32 [2, 256, 256], replicated
- grad_ln2_gain: float32 [2, 256], replicated
- grad_ln2_bias: float32 [2, 256], replicated
- grad_w_up: float32 [2, 256, 1024], replicated
- grad_w_down: float32 [2, 1024, 256], replicated
Inputs may be any that keep to these rules, and one draw needn't show every extreme that they name: `lengths`: in each aligned group of 16 sequences one has length 1024.
All inputs are finite; a program needn't handle non-finite values.
Results may differ from a plain program's by a relative error of at most 0.018.
The roundings to bfloat16 on the way count: a program that leaves them out, or rounds other values in their place, can miss the bound.
Values may be sent and summed in bfloat16 or wider, within the bound.
A program may use at most 384 MiB of HBM per device.

v0:
```python
import jax
import jax.numpy as jnp
from jax import lax
from jax.sharding import PartitionSpec as P

HEAD_DIM = 128
WINDOW = 128


big_negative = -1e30
local_forms = ("snrd,sncd->snrc", "snrc,sncd->snrd", "snrc,snrd->sncd")
strided_forms = ("snod,smod->snmo", "snmo,smod->snod", "snmo,snod->smod")


def shifted(block, axis, distance):
    devices = range(lax.axis_size(axis))
    route = [(i - distance, i) for i in devices if i - distance in devices]
    return lax.ppermute(block, axis, route)


def layer_norm(values, gain, shift):
    center = values - jnp.mean(values, axis=-1, keepdims=True)
    spread = jnp.mean(center * center, axis=-1, keepdims=True)
    return center * lax.rsqrt(spread + 1e-05) * gain + shift


def local_mask(seq_lengths, first_pos, block_count):
    block_start = first_pos + jnp.arange(block_count, dtype=jnp.int32) * WINDOW
    query_pos = block_start[:, None, None] + jnp.arange(WINDOW, dtype=jnp.int32)[None, :, None]
    key_pos = (
        block_start[:, None, None] - WINDOW + jnp.arange(2 * WINDOW, dtype=jnp.int32)[None, None, :]
    )
    allowed = (key_pos <= query_pos) & (key_pos > query_pos - WINDOW) & (key_pos >= 0)
    return allowed[None] & (
        (key_pos[None] < seq_lengths[:, None, None, None]) | (key_pos == query_pos)[None]
    )


def strided_mask(seq_lengths, first_pos, block_count, key_blocks):
    query_block = (first_pos // WINDOW + jnp.arange(block_count, dtype=jnp.int32))[:, None, None]
    key_block = jnp.arange(key_blocks, dtype=jnp.int32)[None, :, None]
    key_pos = key_block * WINDOW + jnp.arange(WINDOW, dtype=jnp.int32)[None, None, :]
    return (key_block <= query_block)[None] & (
        (key_pos[None] < seq_lengths[:, None, None, None]) | (key_block == query_block)[None]
    )


def attend_forward(queries, keys_values, allowed, score_scale, einsum_forms, axis_pick):
    key_part = keys_values[..., :HEAD_DIM]
    value_part = keys_values[..., HEAD_DIM:]
    scores = (
        jnp.einsum(einsum_forms[0], queries, key_part, preferred_element_type=jnp.float32)
        * score_scale
    )
    masked = jnp.where(allowed, scores, big_negative)
    row_peak = jnp.max(masked, axis=axis_pick, keepdims=True)
    powered = jnp.where(allowed, jnp.exp(masked - row_peak), 0.0)
    totals = jnp.sum(powered, axis=axis_pick, keepdims=True)
    weights = (powered / totals).astype(jnp.bfloat16)
    result_rows = jnp.einsum(
        einsum_forms[1], weights, value_part, preferred_element_type=jnp.float32
    )
    return (result_rows, row_peak + jnp.log(totals))


def attend_backward(
    queries, keys_values, allowed, score_scale, log_total, grad_out, einsum_forms, axis_pick
):
    key_part = keys_values[..., :HEAD_DIM]
    value_part = keys_values[..., HEAD_DIM:]
    scores = (
        jnp.einsum(einsum_forms[0], queries, key_part, preferred_element_type=jnp.float32)
        * score_scale
    )
    weights = jnp.where(allowed, jnp.exp(jnp.where(allowed, scores, big_negative) - log_total), 0.0)
    grad_values = jnp.einsum(
        einsum_forms[2], weights.astype(jnp.bfloat16), grad_out, preferred_element_type=jnp.float32
    )
    grad_weights = jnp.einsum(
        einsum_forms[0], grad_out, value_part, preferred_element_type=jnp.float32
    )
    inner = jnp.sum(grad_weights * weights, axis=axis_pick, keepdims=True)
    grad_scores = (weights * (grad_weights - inner)).astype(jnp.bfloat16)
    grad_query = (
        jnp.einsum(einsum_forms[1], grad_scores, key_part, preferred_element_type=jnp.float32)
        * score_scale
    )
    grad_keys = (
        jnp.einsum(einsum_forms[2], grad_scores, queries, preferred_element_type=jnp.float32)
        * score_scale
    )
    return (grad_query, jnp.concatenate([grad_keys, grad_values], axis=-1))


def local_blocks(own_rows, edge_rows):
    seq_count, block_rows, channels = own_rows.shape
    blocks = own_rows.reshape(seq_count, block_rows // WINDOW, WINDOW, channels)
    earlier = jnp.concatenate([edge_rows[:, None], blocks[:, :-1]], axis=1)
    return jnp.concatenate([earlier, blocks], axis=2)


def layer_forward(stream, seq_lengths, first_pos, layer_weights, score_scale):
    gain_one, shift_one, w_pack, w_mix, gain_two, shift_two, w_expand, w_shrink = layer_weights
    seq_count, block_rows, model_width = stream.shape
    block_count = block_rows // WINDOW
    normed = (
        layer_norm(stream, gain_one, shift_one)
        .astype(jnp.bfloat16)
        .reshape(seq_count * block_rows, model_width)
    )
    packed = jnp.dot(normed, w_pack, preferred_element_type=jnp.float32).astype(jnp.bfloat16)
    packed = packed.reshape(seq_count, block_rows, 3, 2, HEAD_DIM)
    near_own = jnp.concatenate([packed[:, :, 1, 0], packed[:, :, 2, 0]], axis=-1)
    edge_rows = shifted(near_own, "wide", 1)
    far_own = jnp.concatenate([packed[:, :, 1, 1], packed[:, :, 2, 1]], axis=-1)
    far_all = lax.all_gather(far_own, "wide", axis=1, tiled=True)
    key_blocks = far_all.shape[1] // WINDOW
    far_keys = far_all.reshape(seq_count, key_blocks, WINDOW, 2 * HEAD_DIM)
    far_mask = strided_mask(seq_lengths, first_pos, block_count, key_blocks)
    far_query = packed[:, :, 0, 1].reshape(seq_count, block_count, WINDOW, HEAD_DIM)
    far_out, far_log = attend_forward(far_query, far_keys, far_mask, score_scale, strided_forms, 2)
    near_keys = local_blocks(near_own, edge_rows)
    near_mask = local_mask(seq_lengths, first_pos, block_count)
    near_query = packed[:, :, 0, 0].reshape(seq_count, block_count, WINDOW, HEAD_DIM)
    near_out, near_log = attend_forward(
        near_query, near_keys, near_mask, score_scale, local_forms, 3
    )
    mixed_heads = jnp.concatenate(
        [near_out.reshape(-1, HEAD_DIM), far_out.reshape(-1, HEAD_DIM)], axis=-1
    ).astype(jnp.bfloat16)
    after_attn = stream + jnp.dot(mixed_heads, w_mix, preferred_element_type=jnp.float32).reshape(
        seq_count, block_rows, model_width
    )
    normed_two = (
        layer_norm(after_attn, gain_two, shift_two).astype(jnp.bfloat16).reshape(-1, model_width)
    )
    hidden = jnp.dot(normed_two, w_expand, preferred_element_type=jnp.float32)
    active = jax.nn.gelu(hidden).astype(jnp.bfloat16)
    result = after_attn + jnp.dot(active, w_shrink, preferred_element_type=jnp.float32).reshape(
        seq_count, block_rows, model_width
    )
    kept_values = (
        stream,
        normed,
        packed,
        near_keys,
        far_query,
        far_keys,
        near_mask,
        far_mask,
        near_log,
        far_log,
        mixed_heads,
        after_attn,
        normed_two,
        hidden,
        active,
    )
    return (result, kept_values)


def layer_backward(grad_result, kept_values, layer_weights, score_scale):
    gain_one, shift_one, w_pack, w_mix, gain_two, shift_two, w_expand, w_shrink = layer_weights
    (
        stream,
        normed,
        packed,
        near_keys,
        far_query,
        far_keys,
        near_mask,
        far_mask,
        near_log,
        far_log,
        mixed_heads,
        after_attn,
        normed_two,
        hidden,
        active,
    ) = kept_values
    seq_count, block_rows, model_width = stream.shape
    block_count = block_rows // WINDOW
    grad_branch = grad_result.reshape(-1, model_width).astype(jnp.bfloat16)
    grad_shrink = jnp.dot(active.T, grad_branch, preferred_element_type=jnp.float32)
    grad_active = jnp.dot(grad_branch, w_shrink.T, preferred_element_type=jnp.float32)
    gelu_pull = jax.vjp(jax.nn.gelu, hidden)[1]
    grad_hidden = gelu_pull(grad_active)[0].astype(jnp.bfloat16)
    grad_expand = jnp.dot(normed_two.T, grad_hidden, preferred_element_type=jnp.float32)
    grad_normed_two = jnp.dot(grad_hidden, w_expand.T, preferred_element_type=jnp.float32).reshape(
        seq_count, block_rows, model_width
    )
    norm_pull_two = jax.vjp(layer_norm, after_attn, gain_two, shift_two)[1]
    back_stream, grad_gain_two, grad_shift_two = norm_pull_two(grad_normed_two)
    grad_after = grad_result + back_stream
    grad_attn = grad_after.reshape(-1, model_width).astype(jnp.bfloat16)
    grad_mix = jnp.dot(mixed_heads.T, grad_attn, preferred_element_type=jnp.float32)
    grad_mixed = jnp.dot(grad_attn, w_mix.T, preferred_element_type=jnp.float32).astype(
        jnp.bfloat16
    )
    near_grad_out = grad_mixed[:, :HEAD_DIM].reshape(seq_count, block_count, WINDOW, HEAD_DIM)
    far_grad_rows = grad_mixed[:, HEAD_DIM:].reshape(seq_count, block_count, WINDOW, HEAD_DIM)
    near_query = packed[:, :, 0, 0].reshape(seq_count, block_count, WINDOW, HEAD_DIM)
    near_grad_query, near_grad_pairs = attend_backward(
        near_query, near_keys, near_mask, score_scale, near_log, near_grad_out, local_forms, 3
    )
    owner_query, far_grad_pairs = attend_backward(
        far_query, far_keys, far_mask, score_scale, far_log, far_grad_rows, strided_forms, 2
    )
    far_grad_query = owner_query.reshape(seq_count, block_rows, HEAD_DIM)
    far_grad_kv = lax.psum_scatter(
        far_grad_pairs.reshape(seq_count, -1, 2 * HEAD_DIM).astype(jnp.bfloat16),
        "wide",
        scatter_dimension=1,
        tiled=True,
    ).astype(jnp.float32)
    earlier_part = near_grad_pairs[:, :, :WINDOW]
    returned = shifted(earlier_part[:, 0].astype(jnp.bfloat16), "wide", -1).astype(jnp.float32)
    own_part = near_grad_pairs[:, :, WINDOW:] + jnp.concatenate(
        [earlier_part[:, 1:], returned[:, None]], axis=1
    )
    near_grad_kv = own_part.reshape(seq_count, block_rows, 2 * HEAD_DIM)
    grad_queries = jnp.concatenate(
        [near_grad_query.reshape(seq_count, block_rows, HEAD_DIM), far_grad_query], axis=-1
    )
    grad_key_rows = jnp.concatenate(
        [near_grad_kv[..., :HEAD_DIM], far_grad_kv[..., :HEAD_DIM]], axis=-1
    )
    grad_value_rows = jnp.concatenate(
        [near_grad_kv[..., HEAD_DIM:], far_grad_kv[..., HEAD_DIM:]], axis=-1
    )
    grad_packed = (
        jnp.stack([grad_queries, grad_key_rows, grad_value_rows], axis=2)
        .reshape(-1, 3 * model_width)
        .astype(jnp.bfloat16)
    )
    grad_pack = jnp.dot(normed.T, grad_packed, preferred_element_type=jnp.float32)
    grad_normed = jnp.dot(grad_packed, w_pack.T, preferred_element_type=jnp.float32).reshape(
        seq_count, block_rows, model_width
    )
    norm_pull_one = jax.vjp(layer_norm, stream, gain_one, shift_one)[1]
    back_input, grad_gain_one, grad_shift_one = norm_pull_one(grad_normed)
    gradients = (
        grad_gain_one,
        grad_shift_one,
        grad_pack,
        grad_mix,
        grad_gain_two,
        grad_shift_two,
        grad_expand,
        grad_shrink,
    )
    return (grad_after + back_input, gradients)


def per_device(
    inputs, lengths, ln1_gain, ln1_bias, w_qkv, w_out, ln2_gain, ln2_bias, w_up, w_down, cotangent
):
    seq_count, block_rows, model_width = inputs.shape
    first_pos = lax.axis_index("wide") * block_rows
    score_scale = float(HEAD_DIM) ** (-0.5)
    stacks = (ln1_gain, ln1_bias, w_qkv, w_out, ln2_gain, ln2_bias, w_up, w_down)
    layer_count = w_qkv.shape[0]
    stream = inputs.astype(jnp.float32)
    inputs_kept = []
    for layer_index in range(layer_count):
        layer_weights = tuple((member[layer_index] for member in stacks))
        inputs_kept.append(stream)
        stream, kept_values = layer_forward(stream, lengths, first_pos, layer_weights, score_scale)
    outputs = stream.astype(jnp.bfloat16)
    grad_stream = cotangent.astype(jnp.float32)
    per_layer = [None] * layer_count
    for layer_index in reversed(range(layer_count)):
        layer_weights = tuple((member[layer_index] for member in stacks))
        kept_values = layer_forward(
            inputs_kept[layer_index], lengths, first_pos, layer_weights, score_scale
        )[1]
        grad_stream, layer_grads = layer_backward(
            grad_stream, kept_values, layer_weights, score_scale
        )
        per_layer[layer_index] = layer_grads
    stacked = tuple(
        (
            jnp.stack([per_layer[position][member] for position in range(layer_count)])
            for member in range(8)
        )
    )
    summed = lax.psum(stacked, ("batch", "wide"))
    return (
        outputs,
        grad_stream,
        summed[0],
        summed[1],
        summed[2],
        summed[3],
        summed[4],
        summed[5],
        summed[6],
        summed[7],
    )


def solution(mesh):
    return jax.shard_map(
        per_device,
        mesh=mesh,
        in_specs=(
            P("batch", "wide", None),
            P("batch"),
            P(),
            P(),
            P(),
            P(),
            P(),
            P(),
            P(),
            P(),
            P("batch", "wide", None),
        ),
        out_specs=(
            P("batch", "wide", None),
            P("batch", "wide", None),
            P(),
            P(),
            P(),
            P(),
            P(),
            P(),
            P(),
            P(),
        ),
        check_vma=False,
    )
```

profile of v0, /device:TPU:1, one launch (start us, length us, event | category | flops | bytes accessed | tf_op | source)
XLA Modules:
  0.0 818.8 jit_solution(11941819341589177898)
XLA Ops:
  17.9 6.9 reshape.855
  24.7 8.3 %fusion.191 = (bf16[16,128,1,1,128]{4,3,2,1,0:T(2,128)(2,1)S(1)}, bf16[16,128,1,1,128]{4,3,2,1,0:T(2,128)(2,1)S(1)}, bf16[16,128,1,1,128]{4,3,2,1,0:T(2,128)(2,1...) fusion(bf16[16,128,3,2,128]{4,3,2,1,0:T(2,128)(2,1)} %reshape.855), kind=kLoop, calls=%fused_computation.348 | loop fusion | bytes 6291456 | tf_op jit(solution)/shard_map/slice | solution.py:113
  43.3 22.4 %collective-permute-done = bf16[16,128,256]{2,1,0:T(8,128)(2,1)} collective-permute-done((bf16[16,128,256]{2,1,0:T(8,128)(2,1)}, bf16[16,128,256]{2,1,0:T(8,128)(2,1)}, u32[]{:S(2)}, u32[]{:S(2)}) %collective-permute-start) | collective-permute-done | bytes 1048608 | tf_op jit(solution)/shard_map/ppermute | solution.py:18
  71.6 48.7 %all-gather.3.cloned.1.call-done = bf16[16,1024,256]{2,1,0:T(8,128)(2,1)} async-done(((bf16[16,128,256]{2,1,0:T(8,128)(2,1)}), bf16[16,1024,256]{2,1,0:T(8,128)(2,1)}) %all-gather.3.cloned.1.call-update) | async-done | bytes 8388624 | tf_op jit(solution)/shard_map/all_gather | solution.py:116
  120.2 5.4 fusion.189
  131.6 6.2 fusion.28
  140.6 5.3 multiply_convert_fusion.5
  152.9 6.9 reshape.865
  159.8 8.3 %fusion.190 = (bf16[16,128,1,1,128]{4,3,2,1,0:T(2,128)(2,1)}, bf16[16,128,1,1,128]{4,3,2,1,0:T(2,128)(2,1)S(1)}, bf16[16,128,1,1,128]{4,3,2,1,0:T(2,128)(2,1)S(1...) fusion(bf16[16,128,3,2,128]{4,3,2,1,0:T(2,128)(2,1)} %reshape.865), kind=kLoop, calls=%fused_computation.347 | loop fusion | bytes 6291456 | tf_op jit(solution)/shard_map/slice | solution.py:113
  172.8 5.9 collective-permute-start.1
  182.8 25.3 %collective-permute-done.1 = bf16[16,128,256]{2,1,0:T(8,128)(2,1)} collective-permute-done((bf16[16,128,256]{2,1,0:T(8,128)(2,1)}, bf16[16,128,256]{2,1,0:T(8,128)(2,1)}, u32[]{:S(2)}, u32[]{:S(2)}) %collective-permute-start.1) | collective-permute-done | bytes 1048608 | tf_op jit(solution)/shard_map/ppermute | solution.py:18
  214.9 43.6 %all-gather.5.cloned.1.call-done = bf16[16,1024,256]{2,1,0:T(8,128)(2,1)} async-done(((bf16[16,128,256]{2,1,0:T(8,128)(2,1)}), bf16[16,1024,256]{2,1,0:T(8,128)(2,1)}) %all-gather.5.cloned.1.call-update) | async-done | bytes 8388624 | tf_op jit(solution)/shard_map/all_gather | solution.py:116
  258.5 5.5 fusion.188
  273.8 6.1 fusion.24
  287.2 6.7 fusion.13
  318.0 7.5 pad_maximum_fusion
  325.5 18.9 %copy.137 = bf16[16,8,128,256]{3,0,2,1:T(8,128)(2,1)} copy(bf16[16,8,128,256]{2,1,3,0:T(8,128)(2,1)} %pad_maximum_fusion) | data formatting | bytes 16777216
  344.4 12.3 %copy.157 = bf16[128,8,16,256]{3,1,2,0:T(8,128)(2,1)} copy(bf16[128,8,16,256]{3,2,1,0:T(8,128)(2,1)} %bitcast.464) | data formatting | bytes 16777216
  379.1 30.8 %collective-permute-done.2 = bf16[16,128,256]{1,2,0:T(8,128)(2,1)} collective-permute-done((bf16[16,128,256]{1,2,0:T(8,128)(2,1)}, bf16[16,128,256]{1,2,0:T(8,128)(2,1)}, u32[]{:S(2)}, u32[]{:S(2)}) %collective-permute-start.2) | collective-permute-done | bytes 1048608 | tf_op jit(solution)/shard_map/ppermute | solution.py:18
  412.4 46.2 %reduce-scatter.7.cloned.1.call-done = bf16[128,4096]{1,0:T(8,128)(2,1)} async-done(((bf16[1024,4096]{1,0:T(8,128)(2,1)}), bf16[128,4096]{1,0:T(8,128)(2,1)}) %reduce-scatter.7.cloned.1.call-update) | async-done | bytes 1048592
  475.3 6.4 fusion.6
  500.0 7.6 pad_maximum_fusion.1
  507.6 19.0 %copy.138 = bf16[16,8,128,256]{3,0,2,1:T(8,128)(2,1)} copy(bf16[16,8,128,256]{2,1,3,0:T(8,128)(2,1)} %pad_maximum_fusion.1) | data formatting | bytes 16777216
  526.6 12.3 %copy.159 = bf16[128,8,16,256]{3,1,2,0:T(8,128)(2,1)} copy(bf16[128,8,16,256]{3,2,1,0:T(8,128)(2,1)} %bitcast.465) | data formatting | bytes 16777216
  541.9 4.6 convolution_bitcast_fusion.4
  546.5 4.7 convolution_bitcast_fusion.2
  566.0 5.9 collective-permute-start.3
  586.7 19.2 %collective-permute-done.3 = bf16[16,128,256]{1,2,0:T(8,128)(2,1)S(1)} collective-permute-done((bf16[16,128,256]{1,2,0:T(8,128)(2,1)S(1)}, bf16[16,128,256]{1,2,0:T(8,128)(2,1)S(1)}, u32[]{:S(2)}, u32[]{:S(2)}) %collective-permute-start.3) | collective-permute-done | bytes 1048608 | tf_op jit(solution)/shard_map/ppermute | solution.py:18
  607.0 31.1 %reduce-scatter.9.cloned.1.call-done = bf16[128,4096]{1,0:T(8,128)(2,1)} async-done(((bf16[1024,4096]{1,0:T(8,128)(2,1)}), bf16[128,4096]{1,0:T(8,128)(2,1)}) %reduce-scatter.9.cloned.1.call-update) | async-done | bytes 1048592
  659.5 41.0 %all-reduce = (f32[2,256]{1,0:T(2,128)}, f32[2,256]{1,0:T(2,128)}, f32[2,256]{1,0:T(2,128)}, f32[2,256]{1,0:T(2,128)}) all-reduce(f32[2,256]{1,0:T(2,128)S(1)} %pad_maximum_fusion.16, f32[2,256]{1,0:T(2,128)S(1)} %pad_maximum_fusion.17, f32[2,256]{1,0:T(2,128)S(1)} %pad_maximum_fusion.18, ...), channel_id=1, replica_groups=mesh['batch'=4,'wide'=8] {'batch','wide'}, use_global_device_ids=true, to_apply=%region_32.33 | all-reduce | flops 2048 | bytes 16384 | tf_op jit(solution)/shard_map/psum | solution.py:287
  700.5 4.9 add_add_fusion.4
  705.4 99.4 %all-reduce.4.cloned.1.call-done = (f32[2,256,768]{2,1,0:T(8,128)}, f32[2,256,256]{2,1,0:T(8,128)}, f32[2,256,1024]{2,1,0:T(8,128)}, f32[2,1024,256]{2,1,0:T(8,128)}) async-done(((f32[2,256,768]{2,1,0:T(8,128)}, f32[2,256,256]{2,1,0:T(8,128)}, f32[2,256,1024]{2,1,0:T(8,128)}, f32[2,1024,256]{2,1,0:T(8,128)}), (f32[2,256,768]{2,1,0:T(8,128)}, f32[2,256,256]{2,1,0:T(8,128)}, f32[2,256,1024]{2,1,0:T(8,128)}, ...) | async-done | bytes 6291472 | tf_op jit(solution)/shard_map/psum | solution.py:287
  (474 shorter events, 219.4 us)
Async XLA Ops:
  7.2 113.0 %all-gather.3.cloned.1.call-start = ((), (), s32[]{:S(2)}) async-start(), calls=%async_computation.2 | async-start | bytes 9437184 | tf_op jit(solution)/shard_map/all_gather | solution.py:116
  34.3 224.2 %all-gather.5.cloned.1.call-start = ((), (), s32[]{:S(2)}) async-start(), calls=%async_computation.3 | async-start | bytes 9437184 | tf_op jit(solution)/shard_map/all_gather | solution.py:116
  34.5 6.5 copy-start.126
  34.6 7.2 copy-start.99
  34.6 7.4 copy-start.30
  35.8 32.4 %copy-start.37 = (bf16[16,1,128,256]{3,2,0,1:T(8,128)(2,1)}, bf16[16,1,128,256]{3,2,0,1:T(8,128)(2,1)S(1)}, u32[]{:S(2)}) copy-start(bf16[16,1,128,256]{3,2,0,1:T(8,128)(2,1)S(1)} %get-tuple-element.76) | copy-start | bytes 3145732
  35.8 29.9 %collective-permute-start = (bf16[16,128,256]{2,1,0:T(8,128)(2,1)}, bf16[16,128,256]{2,1,0:T(8,128)(2,1)}, u32[]{:S(2)}, u32[]{:S(2)}) collective-permute-start(bf16[16,128,256]{2,1,0:T(8,128)(2,1)} %get-tuple-element.77), channel_id=1, source_target_pairs={{0,1},{1,2},{2,3},{3,4},{4,5},{5,6},{6,7},{8,9},{9,10},{10,11},{11... | collective-permute-start | bytes 3145736 | tf_op jit(solution)/shard_map/ppermute | solution.py:18
  40.4 25.3 %copy-start.51 = (bf16[16,128,1,1,128]{4,3,2,1,0:T(2,128)(2,1)S(1)}, bf16[16,128,1,1,128]{4,3,2,1,0:T(2,128)(2,1)}, u32[]{:S(2)}) copy-start(bf16[16,128,1,1,128]{4,3,2,1,0:T(2,128)(2,1)} %get-tuple-element.56) | copy-start | bytes 1572868
  40.5 229.8 %copy-start.103 = (pred[8]{0:T(512)(128)(4,1)}, pred[8]{0:T(512)(128)(4,1)S(1)}, u32[]{:S(2)}) copy-start(pred[8]{0:T(512)(128)(4,1)S(1)} %get-tuple-element.119) | copy-start | bytes 28
  40.5 267.7 %copy-start.101 = (pred[8]{0:T(512)(128)(4,1)}, pred[8]{0:T(512)(128)(4,1)S(1)}, u32[]{:S(2)}) copy-start(pred[8]{0:T(512)(128)(4,1)S(1)} %get-tuple-element.118) | copy-start | bytes 28
  41.1 98.2 %copy-start.118 = (f32[1,256]{1,0:T(1,128)}, f32[1,256]{1,0:T(1,128)S(1)}, u32[]{:S(2)}) copy-start(f32[1,256]{1,0:T(1,128)S(1)} %get-tuple-element.81) | copy-start | bytes 3076
  129.2 8.5 %copy-start.54 = (f32[16,128,1,8]{1,3,0,2:T(8,128)}, f32[16,128,1,8]{1,3,0,2:T(8,128)S(1)}, u32[]{:S(2)}) copy-start(f32[16,128,1,8]{1,3,0,2:T(8,128)S(1)} %copy.97) | copy-start | bytes 196612
  138.6 7.3 copy-start
  139.3 6.6 copy-start.95
  169.5 289.1 %reduce-scatter.7.cloned.1.call-start = ((), (), s32[]{:S(2)}) async-start(), calls=%async_computation.4 | async-start | bytes 9437184
  172.8 35.3 %collective-permute-start.1 = (bf16[16,128,256]{2,1,0:T(8,128)(2,1)}, bf16[16,128,256]{2,1,0:T(8,128)(2,1)}, u32[]{:S(2)}, u32[]{:S(2)}) collective-permute-start(bf16[16,128,256]{2,1,0:T(8,128)(2,1)} %get-tuple-element.75), channel_id=1, source_target_pairs={{0,1},{1,2},{2,3},{3,4},{4,5},{5,6},{6,7},{8,9},{9,10},{10,11},{11... | collective-permute-start | bytes 3145736 | tf_op jit(solution)/shard_map/ppermute | solution.py:18
  180.0 28.1 %copy-start.39 = (bf16[16,1,128,256]{3,2,0,1:T(8,128)(2,1)S(1)}, bf16[16,1,128,256]{3,2,0,1:T(8,128)(2,1)}, u32[]{:S(2)}) copy-start(bf16[16,1,128,256]{3,2,0,1:T(8,128)(2,1)} %get-tuple-element.74) | copy-start | bytes 3145732
  280.9 15.4 %copy-start.8 = (f32[16,128,256]{2,1,0:T(8,128)}, f32[16,128,256]{2,1,0:T(8,128)S(1)}, u32[]{:S(2)}) copy-start(f32[16,128,256]{2,1,0:T(8,128)S(1)} %get-tuple-element.101) | copy-start | bytes 6291460
  356.8 281.3 %reduce-scatter.9.cloned.1.call-start = ((), (), s32[]{:S(2)}) async-start(), calls=%async_computation.5 | async-start | bytes 9437184
  362.5 7.9 slice-start.2
  367.9 42.0 %collective-permute-start.2 = (bf16[16,128,256]{1,2,0:T(8,128)(2,1)}, bf16[16,128,256]{1,2,0:T(8,128)(2,1)}, u32[]{:S(2)}, u32[]{:S(2)}) collective-permute-start(bf16[16,128,256]{1,2,0:T(8,128)(2,1)} %fusion.70), channel_id=1, source_target_pairs={{1,0},{2,1},{3,2},{4,3},{5,4},{6,5},{7,6},{9,8},{10,9},{11,10},{12... | collective-permute-start | bytes 3145736 | tf_op jit(solution)/shard_map/ppermute | solution.py:18
  376.8 33.1 %copy-start.17 = (f32[16,1,256,128]{2,3,0,1:T(8,128)S(1)}, f32[16,1,256,128]{2,3,0,1:T(8,128)}, u32[]{:S(2)}) copy-start(f32[16,1,256,128]{2,3,0,1:T(8,128)} %copy-done.16) | copy-start | bytes 6291460
  378.8 31.1 %copy-start.15 = (f32[16,1,256,128]{2,3,0,1:T(8,128)S(1)}, f32[16,1,256,128]{2,3,0,1:T(8,128)}, u32[]{:S(2)}) copy-start(f32[16,1,256,128]{2,3,0,1:T(8,128)} %copy-done.14) | copy-start | bytes 6291460
  475.2 6.5 copy-start.69
  475.2 10.6 %copy-start.20 = (f32[16,128,256]{2,1,0:T(8,128)}, f32[16,128,256]{2,1,0:T(8,128)S(1)}, u32[]{:S(2)}) copy-start(f32[16,128,256]{2,1,0:T(8,128)S(1)} %get-tuple-element.37) | copy-start | bytes 6291460
  539.0 265.8 %all-reduce.4.cloned.1.call-start = ((), (), s32[]{:S(2)}) async-start(), calls=%async_computation.6 | async-start | bytes 12582912 | tf_op jit(solution)/shard_map/psum | solution.py:287
  541.8 13.0 %slice-start = ((s8[8388608]{0:T(1024)(128)(4,1)}), s8[4194304]{0:T(1024)(128)(4,1)S(1)}, s32[]{:S(2)}) async-start(s8[8388608]{0:T(1024)(128)(4,1)} %bitcast.467), calls=%async_computation.7 | async-start | bytes 8388608
  546.5 8.3 %slice-start.1 = ((s8[8388608]{0:T(1024)(128)(4,1)}), s8[4194304]{0:T(1024)(128)(4,1)S(1)}, s32[]{:S(2)}) async-start(s8[8388608]{0:T(1024)(128)(4,1)} %bitcast.467), calls=%async_computation.8 | async-start | bytes 8388608
  566.0 7.6 copy-start.41
  566.0 39.9 %collective-permute-start.3 = (bf16[16,128,256]{1,2,0:T(8,128)(2,1)S(1)}, bf16[16,128,256]{1,2,0:T(8,128)(2,1)S(1)}, u32[]{:S(2)}, u32[]{:S(2)}) collective-permute-start(bf16[16,128,256]{1,2,0:T(8,128)(2,1)S(1)} %fusion.71), channel_id=1, source_target_pairs={{1,0},{2,1},{3,2},{4,3},{5,4},{6,5},{7,6},{9,8},{10,9},{11,10},{12... | collective-permute-start | bytes 3145736 | tf_op jit(solution)/shard_map/ppermute | solution.py:18
  656.9 43.7 %copy-start.19 = (f32[16,128,256]{2,1,0:T(8,128)S(1)}, f32[16,128,256]{2,1,0:T(8,128)}, u32[]{:S(2)}) copy-start(f32[16,128,256]{2,1,0:T(8,128)} %copy-done.18) | copy-start | bytes 6291460
  656.9 43.7 %copy-start.98 = (f32[16,128]{1,0:T(8,128)S(1)}, f32[16,128]{1,0:T(8,128)}, u32[]{:S(2)}) copy-start(f32[16,128]{1,0:T(8,128)} %copy-done.97) | copy-start | bytes 24580
  (120 other events, 328.6 us)
Sparse Core Ops, SparseCore 0:
  34.4 85.7 all-gather.2
  169.6 88.8 all-gather.4
  356.9 101.6 reduce-scatter.6
  539.1 98.9 reduce-scatter.8
  646.9 157.8 all-reduce.3
where the time goes:
time: 829 us; the launch traced here: 819 us
  waiting for transfers between devices  367 us (44%)
  local copies, waits for them, and re-layouts  183 us (22%)
  matrix products  109 us (13%)
  other arithmetic  83.6 us (10%)
  blocking collectives  41 us (5%)
  starting transfers between devices  19 us (2%)
  between operations  16.1 us (2%)
    unnamed x304, local copies, waits for them, and re-layouts  105 us
    psum x1, waiting for transfers between devices, per_device(): summed = lax.psum(stacked, ('batch', 'wide'))  99.4 us
    ppermute x4, waiting for transfers between devices, shifted(): return lax.ppermute(block, axis, route)  97.8 us
    all_gather x2, waiting for transfers between devices, layer_forward(): far_all = lax.all_gather(far_own, 'wide', axis=1, tiled=True)  92.3 us
    unnamed x7, waiting for transfers between devices  77.4 us
    psum x1, blocking collectives, per_device(): summed = lax.psum(stacked, ('batch', 'wide'))  41 us
    ppermute x4, starting transfers between devices, shifted(): return lax.ppermute(block, axis, route)  18.8 us
    dot_general x4, matrix products, attend_forward(): jnp.einsum(einsum_forms[1], weights, value_part, preferred_element_type=j...  17.8 us
  transfers between devices with their start and end apart: 9, of which 9 were waited for; matrix products, arithmetic and copies ran while one was open for 11% of the time, Pallas kernels for 0%

commit v1 on v0

v1 whole, which is shorter than its diff:
```python
import types

import jax
import jax.numpy as jnp
from jax import lax
from jax.experimental import pallas as pl
from jax.experimental.pallas import tpu as pltpu
from jax.sharding import PartitionSpec as P

MESH = pl.DeviceIdType.MESH
F32, BF16 = jnp.float32, jnp.bfloat16
HEAD = 128
WINDOW = 128
GROUP = 16
TILE = 4
PIECE = 32
CHUNK = 256
ROOMY = 8
AT_ONCE = 4
Q_NEAR, Q_FAR, K_NEAR, K_FAR, V_NEAR, V_FAR = (slice(i * HEAD, (i + 1) * HEAD) for i in range(6))
FAR = 1 << 20
MASKED = -1e30
LOG2E = 1.4426950408889634
GELU_A = 0.7978845608028654
GELU_B = GELU_A * 0.044715


def dot(a, b):
    return lax.dot_general(a, b, (((1,), (0,)), ((), ())), preferred_element_type=F32)


def dot_nt(a, b):
    return lax.dot_general(a, b, (((1,), (1,)), ((), ())), preferred_element_type=F32)


def dot_tn(a, b):
    return lax.dot_general(a, b, (((0,), (0,)), ((), ())), preferred_element_type=F32)


def flat(v):
    return v.reshape(-1, v.shape[-1])


def blocks(v):
    return v.reshape(-1, WINDOW, v.shape[-1])


def normalize(x):
    center = x - jnp.mean(x, axis=-1, keepdims=True)
    inverse = lax.rsqrt(jnp.mean(center * center, axis=-1, keepdims=True) + 1e-05)
    return center * inverse, inverse


def norm_back(grad, hat, inverse, gain):
    scaled = grad * gain
    first = jnp.mean(scaled, axis=-1, keepdims=True)
    second = jnp.mean(scaled * hat, axis=-1, keepdims=True)
    return inverse * (scaled - first - hat * second)


def row_sums(v):
    return jnp.sum(v.reshape(-1, 8, v.shape[-1]), axis=0)


def pieces_of(rows):
    return [slice(i, i + PIECE) for i in range(0, rows, PIECE)]


def weights_of(scores, order, limit, factor):
    parts = []
    for r in pieces_of(scores.shape[0]):
        masked = jnp.where(order[r] < limit, scores[r], MASKED)
        peak = jnp.max(masked, axis=1, keepdims=True)
        powered = jnp.exp2((masked - peak) * factor)
        parts.append((powered * (1.0 / jnp.sum(powered, axis=1, keepdims=True))).astype(BF16))
    return jnp.concatenate(parts, axis=0)


def gelu_pair(h):
    square = h * h
    q = 0.5 * jnp.tanh(h * (GELU_B * square + GELU_A)) + 0.5
    g = h * q
    slope = q + g * (1.0 - q) * (6.0 * GELU_B * square + 2.0 * GELU_A)
    return g.astype(BF16), slope.astype(BF16)


def plan(nb, nw, ns, nblk, width, hidden, layers):
    total = ns * nblk
    far_rows = nblk * GROUP
    rows = 12 * CHUNK
    pieces = {}

    def vmem(name, dims, kind):
        pieces[name] = pltpu.VMEM(dims, kind)

    def sems(name, *dims):
        pieces[name] = pltpu.SemaphoreType.DMA(dims)

    vmem("x_in", (total, WINDOW, width), BF16)
    vmem("cot_in", (total, WINDOW, width), BF16)
    vmem("w_qkv", (layers, width, 3 * width), BF16)
    vmem("w_out", (layers, width, width), BF16)
    vmem("w_up", (layers, width, hidden), BF16)
    vmem("w_down", (layers, hidden, width), BF16)
    vmem("a1", (layers, nblk, WINDOW, width), BF16)
    vmem("a2", (layers, nblk, WINDOW, width), BF16)
    vmem("qkv", (layers, nblk, WINDOW, 3 * width), BF16)
    vmem("heads", (layers, nblk, WINDOW, width), BF16)
    vmem("near_p", (layers, nblk, WINDOW, 2 * WINDOW), BF16)
    vmem("far_p", (layers, WINDOW // GROUP, far_rows, far_rows), BF16)
    vmem("act", (layers, nblk, WINDOW, hidden), BF16)
    vmem("slope", (layers, nblk, WINDOW, hidden), BF16)
    vmem("stats", (nblk, WINDOW, WINDOW), F32)
    vmem("dx", (nblk, WINDOW, width), F32)
    vmem("df", (nblk, WINDOW, width), BF16)
    vmem("dm", (nblk, WINDOW, width), BF16)
    vmem("do", (nblk, WINDOW, width), BF16)
    vmem("near_ds", (nblk, WINDOW, 2 * WINDOW), BF16)
    vmem("near_dq", (nblk, WINDOW, HEAD), BF16)
    vmem("df_t", (width, nblk * WINDOW), BF16)
    vmem("heads_t", (width, nblk * WINDOW), BF16)
    if nblk <= ROOMY:
        vmem("a1_t", (layers, width, nblk * WINDOW), BF16)
        vmem("a2_t", (layers, width, nblk * WINDOW), BF16)
        vmem("w_qkv_t", (layers, 3 * width, width), BF16)
        vmem("w_out_t", (layers, width, width), BF16)
        vmem("w_up_t", (layers, hidden, width), BF16)
        vmem("w_down_t", (layers, width, hidden), BF16)
    vmem("near_order", (2, WINDOW, 2 * WINDOW), jnp.int32)
    vmem("far_order", (far_rows, far_rows), jnp.int32)
    vmem("sums", (layers, 4, 8, width), F32)
    vmem("grad", (layers, rows, CHUNK), F32)
    vmem("final", (layers, rows, CHUNK), BF16)
    vmem("got_core", (layers, rows // 2, CHUNK), BF16)
    vmem("got_batch", (layers, nb, rows // 2 // nb, CHUNK), BF16)
    vmem("got_pair", (layers, rows // 4 // nb, CHUNK), BF16)
    top = max(nw.bit_length() - 3, 1)
    vmem("got_top", (layers, top, rows // 4 // nb, CHUNK), BF16)
    vmem("put_core", (hidden, CHUNK), BF16)
    vmem("put_batch", (hidden, CHUNK), BF16)
    vmem("put_pair", (rows // 4 // nb, CHUNK), BF16)
    vmem("put_top", (top, rows // 4 // nb, CHUNK), BF16)
    vmem("norm_all", (nw, 4 * layers, width), F32)
    vmem("norm_batch", (nb, 4 * layers, width), F32)
    for name in ("in", "cot", "out", "gi"):
        sems(name + "_s", ns, nw)
        sems(name + "_r", ns, nw)
    sems("own", 4, ns)
    sems("load", 4)
    sems("save", layers, 2)
    for name, count in (("core", 1), ("batch", nb), ("pair", 1), ("top", top), ("pair_back", 1), ("batch_back", nb), ("core_back", 1)):
        sems(name + "_s", layers, 2, count)
        sems(name + "_r", layers, 2, count)
    sems("norm_all_s", nw)
    sems("norm_all_r", nw)
    sems("norm_batch_s", nb)
    sems("norm_batch_r", nb)
    return pieces


def kernel(nb, nw, ns, names, *refs):
    (lens, x_hbm, cot_hbm, gain1, bias1, gain2, bias2, wq_hbm, wo_hbm, wu_hbm, wd_hbm,
     out_hbm, gi_hbm, grads_hbm, norm_out) = refs[:15]
    m = types.SimpleNamespace(**dict(zip(names, refs[15:])))
    layers, width = gain1.shape
    hidden = wu_hbm.shape[2]
    per = x_hbm.shape[2]
    nblk = nw * per
    tiles = nblk // TILE
    groups = WINDOW // GROUP
    near_each = nblk // groups
    scale = float(HEAD) ** (-0.5)
    factor = scale * LOG2E
    me = lax.axis_index("wide")
    mb = lax.axis_index("batch")

    barrier = pltpu.get_barrier_semaphore()
    for k in range(1, nw):
        pl.semaphore_signal(barrier, inc=1, device_id=(mb, lax.rem(me + k, nw)), device_id_type=MESH)
    for k in range(1, nb):
        pl.semaphore_signal(barrier, inc=1, device_id=(lax.rem(mb + k, nb), me), device_id_type=MESH)
    pl.semaphore_wait(barrier, nw + nb - 2)

    def partner(k):
        place = me
        for bit in range(nw.bit_length() - 1):
            size = 2**bit
            if k & size:
                place = place + size - 2 * size * lax.rem(me // size, 2)
        return place

    far = [nw // 2 + k for k in range(nw // 2)]
    close = [k for k in range(nw // 2 - 1, 0, -1)]
    turns = [turn for pair in zip(far, close) for turn in pair] + [far[-1]]

    def gather_copy(src, dst, send, recv, s, other, owner):
        return pltpu.make_async_remote_copy(
            src_ref=src.at[other, s],
            dst_ref=dst.at[pl.ds(s * nblk + owner * per, per)],
            send_sem=send.at[s, other],
            recv_sem=recv.at[s, owner],
            device_id=(mb, other),
            device_id_type=MESH,
        )

    def gather_own(src, dst, which, s):
        return pltpu.make_async_copy(
            src.at[me, s], dst.at[pl.ds(s * nblk + me * per, per)], m.own.at[which, s]
        )

    def gather_start(src, dst, send, recv, which, s):
        for k in turns:
            gather_copy(src, dst, send, recv, s, partner(k), me).start()
        gather_own(src, dst, which, s).start()

    def gather_wait(src, dst, send, recv, which, s):
        for k in range(1, nw):
            other = partner(k)
            gather_copy(src, dst, send, recv, s, other, other).wait_recv()
        gather_own(src, dst, which, s).wait()

    def gather_end(src, dst, send, recv, s):
        for k in range(1, nw):
            gather_copy(src, dst, send, recv, s, partner(k), me).wait_send()

    def scatter_copy(src, dst, send, recv, s, other, owner):
        return pltpu.make_async_remote_copy(
            src_ref=src.at[pl.ds(s * nblk + other * per, per)],
            dst_ref=dst.at[owner, s],
            send_sem=send.at[s, other],
            recv_sem=recv.at[s, owner],
            device_id=(mb, other),
            device_id_type=MESH,
        )

    def scatter_own(src, dst, which, s):
        return pltpu.make_async_copy(
            src.at[pl.ds(s * nblk + me * per, per)], dst.at[me, s], m.own.at[which, s]
        )

    def scatter_start(src, dst, send, recv, which, s):
        for k in turns:
            scatter_copy(src, dst, send, recv, s, partner(k), me).start()
        scatter_own(src, dst, which, s).start()

    def scatter_end(src, dst, send, recv, which, s):
        for k in range(1, nw):
            scatter_copy(src, dst, send, recv, s, partner(k), me).wait_send()
        for k in range(1, nw):
            other = partner(k)
            scatter_copy(src, dst, send, recv, s, other, other).wait_recv()
        scatter_own(src, dst, which, s).wait()

    ins = (x_hbm, m.x_in, m.in_s, m.in_r)
    cots = (cot_hbm, m.cot_in, m.cot_s, m.cot_r)
    outs = (m.x_in, out_hbm, m.out_s, m.out_r)
    gis = (m.cot_in, gi_hbm, m.gi_s, m.gi_r)

    gather_start(*ins, 0, 0)
    loads = [
        pltpu.make_async_copy(src, dst, m.load.at[i])
        for i, (src, dst) in enumerate(
            ((wq_hbm, m.w_qkv), (wo_hbm, m.w_out), (wu_hbm, m.w_up), (wd_hbm, m.w_down))
        )
    ]
    for load in loads:
        load.start()

    def orders(rows, columns, earlier, same, position):
        row = lax.broadcasted_iota(jnp.int32, (rows, columns), 0)
        column = lax.broadcasted_iota(jnp.int32, (rows, columns), 1)
        own = jnp.where(earlier(row, column), position(column), FAR)
        return jnp.where(same(row, column), -FAR, own)

    def near(lowest):
        return orders(
            WINDOW,
            2 * WINDOW,
            lambda r, c: (c < r + WINDOW) & (c > r) & (c >= lowest),
            lambda r, c: c == r + WINDOW,
            lambda c: c,
        )

    m.near_order[0] = near(WINDOW)
    m.near_order[1] = near(0)
    far_rows = nblk * GROUP
    m.far_order[...] = orders(
        far_rows,
        far_rows,
        lambda r, c: (c < r) & (((r - c) & (GROUP - 1)) == 0),
        lambda r, c: c == r,
        lambda c: (c // GROUP) * WINDOW + (c & (GROUP - 1)),
    )
    m.sums[...] = jnp.zeros_like(m.sums)
    for load in loads:
        load.wait()
    roomy = nblk <= ROOMY
    for l in range(layers if roomy else 0):
        m.w_out_t[l] = m.w_out[l].T
        for c in range(3):
            part = slice(c * CHUNK, (c + 1) * CHUNK)
            m.w_qkv_t[l, part] = m.w_qkv[l, :, part].T
        for c in range(hidden // CHUNK):
            part = slice(c * CHUNK, (c + 1) * CHUNK)
            m.w_up_t[l, part] = m.w_up[l, :, part].T
            m.w_down_t[l, :, part] = m.w_down[l, part].T

    def rows_of(t):
        return pl.ds(t * TILE, TILE)

    def back_dot(x, name, l):
        if roomy:
            return dot(x, getattr(m, name + "_t")[l])
        return dot_nt(x, getattr(m, name)[l])

    def lanes_of(t):
        return pl.ds(pl.multiple_of(t * TILE * WINDOW, TILE * WINDOW), TILE * WINDOW)

    def cols(c):
        return slice(c * CHUNK, (c + 1) * CHUNK)

    def loop(count, body, unroll=1):
        unroll = min(unroll, count)

        def step(i, carry):
            for e in range(unroll):
                body(i * unroll + e)
            return carry

        lax.fori_loop(0, count // unroll, step, 0)

    def near_tiles(i):
        return [i * AT_ONCE * near_each + e for e in range(AT_ONCE * near_each)]

    def far_tiles(i):
        return [i * AT_ONCE + e for e in range(AT_ONCE)]

    def window(ref, b, part):
        return jnp.concatenate([ref[jnp.maximum(b - 1, 0), :, part], ref[b, :, part]], axis=0)

    def spread(i):
        return pl.ds(pl.multiple_of(i * GROUP, GROUP), GROUP)

    def strided(v):
        return v.astype(BF16).reshape(nblk, GROUP, HEAD)

    def halves_of(t):
        step = TILE if roomy else 2
        return [pl.ds(t * TILE + i, step) for i in range(0, TILE, step)]

    def parts_of(rows):
        each = WINDOW // PIECE
        return [
            (rows.start + i // each, slice(i % each * PIECE, (i % each + 1) * PIECE), slice(i * PIECE, (i + 1) * PIECE))
            for i in range(rows.size * each)
        ]

    def store_norm(l, which, b, r, x, normed, gain, bias):
        hat, inverse = normalize(x)
        k = 2 * l + which
        m.stats[b, r, k : k + 1] = inverse
        normed[l, b, r] = (hat * gain[l : l + 1] + bias[l : l + 1]).astype(BF16)

    def source(l, s, b, r):
        if l == 0:
            return m.x_in[s * nblk + b, r].astype(F32)
        return m.dx[b, r]

    def forward(l, s):
        length = lens[me * ns + s]

        def project(t):
            for b, r, _ in parts_of(rows_of(t)):
                store_norm(l, 0, b, r, source(l, s, b, r), m.a1, gain1, bias1)
            rows = rows_of(t)
            a = flat(m.a1[l, rows])
            if roomy:
                m.a1_t[l, :, lanes_of(t)] = a.T
            m.qkv[l, rows] = blocks(dot(a, m.w_qkv[l]).astype(BF16))

        here = m.qkv.at[l]

        def attend(i):
            scores = [
                dot_nt(here[b, :, Q_NEAR], window(here, b, K_NEAR)) for b in near_tiles(i)
            ] + [dot_nt(flat(here[:, spread(j), Q_FAR]), flat(here[:, spread(j), K_FAR])) for j in far_tiles(i)]
            rules = [
                (m.near_order.at[jnp.minimum(b, 1)], length - (b - 1) * WINDOW) for b in near_tiles(i)
            ] + [(m.far_order, length - j * GROUP) for j in far_tiles(i)]
            p = [weights_of(x, *rule, factor) for x, rule in zip(scores, rules)]
            for b, x in zip(near_tiles(i), p):
                m.near_p[l, b] = x
                result = dot(x, window(here, b, V_NEAR))
                m.heads[l, b, :, 0:HEAD] = result.astype(BF16)
            for j, x in zip(far_tiles(i), p[len(near_tiles(i)) :]):
                m.far_p[l, j] = x
                result = dot(x, flat(here[:, spread(j), V_FAR]))
                m.heads[l, :, spread(j), HEAD:] = strided(result)

        def mix(t):
            rows = rows_of(t)
            mixed = dot(flat(m.heads[l, rows]), m.w_out[l])
            for b, r, i in parts_of(rows_of(t)):
                y = source(l, s, b, r) + mixed[i]
                m.dx[b, r] = y
                store_norm(l, 1, b, r, y, m.a2, gain2, bias2)
            if roomy:
                m.a2_t[l, :, lanes_of(t)] = flat(m.a2[l, rows]).T
            for half in halves_of(t):
                h = dot(flat(m.a2[l, half]), m.w_up[l])
                for b, r, i in parts_of(half):
                    for c in range(hidden // CHUNK):
                        m.act[l, b, r, cols(c)], m.slope[l, b, r, cols(c)] = gelu_pair(h[i, cols(c)])
            fed = dot(flat(m.act[l, rows]), m.w_down[l])
            for b, r, i in parts_of(rows_of(t)):
                y = m.dx[b, r] + fed[i]
                if l == layers - 1:
                    m.x_in[s * nblk + b, r] = y.astype(BF16)
                else:
                    m.dx[b, r] = y

        loop(tiles, project)
        loop(groups // AT_ONCE, attend)
        loop(tiles, mix)

    def unnorm(l, which, b, r, grad, normed, gain, bias, over):
        hat = (normed[l, b, r].astype(F32) - bias[l : l + 1]) * over
        k = 2 * l + which
        back = norm_back(grad, hat, m.stats[b, r, k : k + 1], gain[l : l + 1])
        return back, row_sums(grad * hat), row_sums(grad)

    def add_sums(l, which, terms):
        for k in range(2):
            total = terms[0][k]
            for term in terms[1:]:
                total = total + term[k]
            m.sums[l, 2 * which + k] += total

    def back_feed(l, s):
        def body(t):
            rows = rows_of(t)
            source = m.cot_in.at[pl.ds(s * nblk, nblk)] if l == layers - 1 else m.dx
            for b, r, _ in parts_of(rows_of(t)):
                m.df[b, r] = source[b, r].astype(BF16)
            m.df_t[:, lanes_of(t)] = flat(m.df[rows]).T
            m.heads_t[:, lanes_of(t)] = flat(m.heads[l, rows]).T
            for half in halves_of(t):
                dg = back_dot(flat(m.df[half]), "w_down", l)
                for b, r, i in parts_of(half):
                    for c in range(hidden // CHUNK):
                        slope = m.slope[l, b, r, cols(c)].astype(F32)
                        m.slope[l, b, r, cols(c)] = (dg[i, cols(c)] * slope).astype(BF16)
            da = back_dot(flat(m.slope[l, rows]), "w_up", l)
            over = 1.0 / gain2[l : l + 1]
            terms = []
            for b, r, i in parts_of(rows_of(t)):
                back, *term = unnorm(l, 1, b, r, da[i], m.a2, gain2, bias2, over)
                terms.append(term)
                dy = source[b, r].astype(F32) + back
                m.dx[b, r] = dy
                m.dm[b, r] = dy.astype(BF16)
            add_sums(l, 1, terms)
            do = back_dot(flat(m.dm[rows]), "w_out", l)
            m.do[pl.ds(t * TILE, TILE)] = blocks(do.astype(BF16))

        loop(tiles, body)

    def back_scores(p, dp):
        parts = []
        for r in pieces_of(dp.shape[0]):
            high = p[r].astype(F32)
            inner = jnp.sum(dp[r] * high, axis=1, keepdims=True)
            parts.append((high * (dp[r] - inner)).astype(BF16))
        return jnp.concatenate(parts, axis=0)

    def back_attend(l, s):
        here = m.qkv.at[l]
        near_p = m.near_p.at[l]

        def body(i):
            near, far = near_tiles(i), far_tiles(i)
            far_do = [flat(m.do[:, spread(j), HEAD:]) for j in far]
            far_p = [m.far_p[l, j] for j in far]
            dp = [dot_nt(m.do[b, :, 0:HEAD], window(here, b, V_NEAR)) for b in near]
            dp += [dot_nt(x, flat(here[:, spread(j), V_FAR])) for j, x in zip(far, far_do)]
            p = [near_p[b] for b in near] + far_p
            ds = [back_scores(x, y) for x, y in zip(p, dp)]
            for b, x in zip(near, ds):
                m.near_ds[b] = x
                m.near_dq[b] = (dot(x, window(here, b, K_NEAR)) * scale).astype(BF16)
            for j, do, w, x in zip(far, far_do, far_p, ds[len(near) :]):
                q = flat(here[:, spread(j), Q_FAR])
                dq = dot(x, flat(here[:, spread(j), K_FAR])) * scale
                dk = dot_tn(x, q) * scale
                dv = dot_tn(w, do)
                here[:, spread(j), Q_FAR] = strided(dq)
                here[:, spread(j), K_FAR] = strided(dk)
                here[:, spread(j), V_FAR] = strided(dv)

        loop(groups // AT_ONCE, body)
        for b in range(nblk):
            if b + 1 < nblk:
                both = slice(b, b + 2)
                ds = jnp.concatenate([m.near_ds[b, :, WINDOW:], m.near_ds[b + 1, :, :WINDOW]], axis=0)
                p = jnp.concatenate([near_p[b, :, WINDOW:], near_p[b + 1, :, :WINDOW]], axis=0)
                q, do = flat(here[both, :, Q_NEAR]), flat(m.do[both, :, 0:HEAD])
            else:
                ds, p = m.near_ds[b, :, WINDOW:], near_p[b, :, WINDOW:]
                q, do = here[b, :, Q_NEAR], m.do[b, :, 0:HEAD]
            here[b, :, K_NEAR] = (dot_tn(ds, q) * scale).astype(BF16)
            here[b, :, V_NEAR] = dot_tn(p, do).astype(BF16)
            here[b, :, Q_NEAR] = m.near_dq[b]

    def back_project(l, s):
        def body(t):
            da = back_dot(flat(m.qkv[l, rows_of(t)]), "w_qkv", l)
            over = 1.0 / gain1[l : l + 1]
            terms = []
            for b, r, i in parts_of(rows_of(t)):
                back, *term = unnorm(l, 0, b, r, da[i], m.a1, gain1, bias1, over)
                terms.append(term)
                if l == 0:
                    m.cot_in[s * nblk + b, r] = (m.dx[b, r] + back).astype(BF16)
                else:
                    m.dx[b, r] = m.dx[b, r] + back
            add_sums(l, 0, terms)

        loop(tiles, body)

    def outer(l, s, left, ref, first, flipped=False):
        if len(left.shape) == 2:
            product = dot(left[...], flat(ref[...]))
        else:
            product = dot_tn(flat(left[...]), flat(ref[...]))
        for c in range(product.shape[1] // CHUNK):
            part = product[:, cols(c)]
            part = part.T if flipped else part
            if s > 0:
                part = part + m.grad[l, cols(first + c)]
            m.grad[l, cols(first + c)] = part

    def grads_feed(l, s):
        outer(l, s, (m.a2_t if roomy else m.a2).at[l], m.slope.at[l], 0)
        outer(l, s, m.df_t, m.act.at[l], hidden // CHUNK, True)

    def grads_attend(l, s):
        first = 2 * hidden // CHUNK
        outer(l, s, m.heads_t, m.dm, first)
        outer(l, s, (m.a1_t if roomy else m.a1).at[l], m.qkv.at[l], first + 1)

    core = lax.rem(me, 2)
    second = lax.rem(me // 2, 2)
    bits = nw.bit_length() - 1

    def toggled(bit):
        size = 2**bit
        return me + size - 2 * size * lax.rem(me // size, 2)

    def reduction(l, which):
        start, count = ((0, 2 * hidden), (2 * hidden, 4 * CHUNK))[which]
        half, chunk, piece = count // 2, count // 2 // nb, count // 4 // nb
        lead = start // 2
        final = m.final.at[l]

        def span(at, size):
            return pl.ds(pl.multiple_of(at, 16), size)

        mine = start + core * half
        theirs = start + (1 - core) * half
        chunk_at = mine + mb * chunk
        piece_at = chunk_at + second * piece
        other_piece = chunk_at + (1 - second) * piece
        core_in = m.got_core.at[l, pl.ds(lead, half)]

        def remote(src, dst, name, k_send, k_recv, device):
            return pltpu.make_async_remote_copy(
                src_ref=src,
                dst_ref=dst,
                send_sem=getattr(m, name + "_s").at[l, which, k_send],
                recv_sem=getattr(m, name + "_r").at[l, which, k_recv],
                device_id=device,
                device_id_type=MESH,
            )

        def here(at, size):
            return final.at[span(at, size)]

        to_core = remote(m.put_core.at[pl.ds(0, half)], core_in, "core", 0, 0, (mb, toggled(0)))
        to_pair = remote(
            m.put_pair.at[pl.ds(start // 4 // nb, piece)],
            m.got_pair.at[l, pl.ds(start // 4 // nb, piece)],
            "pair", 0, 0, (mb, toggled(1)),
        )

        def to_batch(other, owner):
            return remote(
                m.put_batch.at[span(other * chunk, chunk)],
                m.got_batch.at[l, owner, pl.ds(start // 2 // nb, chunk)],
                "batch", other, owner, (other, me),
            )

        def to_top(bit):
            return remote(
                m.put_top.at[bit - 2, pl.ds(start // 4 // nb, piece)],
                m.got_top.at[l, bit - 2, pl.ds(start // 4 // nb, piece)],
                "top", bit - 2, bit - 2, (mb, toggled(bit)),
            )

        def pair_back(at):
            return remote(here(at, piece), here(at, piece), "pair_back", 0, 0, (mb, toggled(1)))

        def batch_back(other, owner):
            at = mine + owner * chunk
            return remote(here(at, chunk), here(at, chunk), "batch_back", other, owner, (other, me))

        def core_back(at):
            return remote(here(at, half), here(at, half), "core_back", 0, 0, (mb, toggled(0)))

        def others():
            return [lax.rem(mb + k, nb) for k in range(1, nb)]

        def step0():
            m.put_core[pl.ds(0, half)] = m.grad[l, span(theirs, half)].astype(BF16)
            to_core.start()

        def step1():
            to_core.wait()
            total = m.grad[l, span(mine, half)] + m.got_core[l, pl.ds(lead, half)].astype(F32)
            m.grad[l, span(mine, half)] = total
            m.put_batch[pl.ds(0, half)] = total.astype(BF16)
            for other in others():
                to_batch(other, mb).start()

        def step2():
            total = m.grad[l, span(chunk_at, chunk)]
            for other in others():
                to_batch(other, mb).wait_send()
                to_batch(other, other).wait_recv()
                got = m.got_batch[l, other, pl.ds(start // 2 // nb, chunk)]
                total = total + got.astype(F32)
            m.grad[l, span(chunk_at, chunk)] = total
            send = m.grad[l, span(other_piece, piece)]
            m.put_pair[pl.ds(start // 4 // nb, piece)] = send.astype(BF16)
            to_pair.start()

        def step3():
            to_pair.wait()
            got = m.got_pair[l, pl.ds(start // 4 // nb, piece)]
            total = m.grad[l, span(piece_at, piece)] + got.astype(F32)
            m.put_top[0, pl.ds(start // 4 // nb, piece)] = total.astype(BF16)
            to_top(2).start()

        def step4(bit=2):
            to_top(bit).wait()
            at = pl.ds(start // 4 // nb, piece)
            total = m.put_top[bit - 2, at].astype(F32) + m.got_top[l, bit - 2, at].astype(F32)
            if bit + 1 < bits:
                m.put_top[bit - 1, at] = total.astype(BF16)
                to_top(bit + 1).start()
                step4(bit + 1)
            else:
                final[span(piece_at, piece)] = total.astype(BF16)
                pair_back(piece_at).start()

        def step5():
            pair_back(other_piece).wait_recv()
            for other in others():
                batch_back(other, mb).start()

        def step6():
            for other in others():
                batch_back(other, other).wait_recv()
            core_back(mine).start()

        save = pltpu.make_async_copy(
            final.at[pl.ds(start, count)],
            grads_hbm.at[l, pl.ds(start, count)],
            m.save.at[l, which],
        )

        def step7():
            core_back(theirs).wait_recv()
            save.start()

        def step8():
            pair_back(piece_at).wait_send()
            for other in others():
                batch_back(other, mb).wait_send()
            core_back(mine).wait_send()
            save.wait()

        return [step0, step1, step2, step3, step4, step5, step6, step7, step8]

    sums = {(l, w): reduction(l, w) for l in range(layers) for w in range(2)}
    waiting = []

    def advance():
        for steps in list(waiting):
            steps.pop(0)()
            if not steps:
                waiting.remove(steps)

    def begin(l, which, last):
        if last:
            steps = sums[l, which]
            steps.pop(0)()
            waiting.append(steps)

    for s in range(ns):
        last = s == ns - 1
        gather_wait(*ins, 0, s)
        if s == 0:
            gather_start(*cots, 1, s)
        for l in range(layers):
            with jax.named_scope("layer_forward"):
                forward(l, s)
        gather_wait(*cots, 1, s)
        if not last:
            gather_start(*ins, 0, s + 1)
        else:
            scatter_start(*outs, 2, s)
        for l in reversed(range(layers)):
            with jax.named_scope("feed_backward"):
                back_feed(l, s)
            if l < layers - 1:
                advance()
            with jax.named_scope("feed_gradients"):
                grads_feed(l, s)
            begin(l, 0, last)
            with jax.named_scope("attention_backward"):
                back_attend(l, s)
            advance()
            if not last:
                if l == layers - 1:
                    gather_start(*cots, 1, s + 1)
                if l == 0:
                    scatter_start(*outs, 2, s)
            with jax.named_scope("attention_gradients"):
                grads_attend(l, s)
            begin(l, 1, last)
            with jax.named_scope("input_backward"):
                back_project(l, s)
            if l == 0:
                advance()
        scatter_start(*gis, 3, s)

    def norm_copy(own, slots, k, device, name, owner):
        return pltpu.make_async_remote_copy(
            src_ref=slots.at[own],
            dst_ref=slots.at[owner],
            send_sem=getattr(m, name + "_s").at[k],
            recv_sem=getattr(m, name + "_r").at[owner],
            device_id=device,
            device_id_type=MESH,
        )

    m.norm_all[me] = jnp.sum(m.sums[...].reshape(4 * layers, 8, width), axis=1)
    for k in range(1, nw):
        other = lax.rem(me + k, nw)
        norm_copy(me, m.norm_all, other, (mb, other), "norm_all", me).start()
    advance()
    for k in range(1, nw):
        other = lax.rem(me + k, nw)
        norm_copy(me, m.norm_all, other, (mb, other), "norm_all", other).wait_recv()
    total = m.norm_all[0]
    for k in range(1, nw):
        total = total + m.norm_all[k]
    m.norm_batch[mb] = total
    for k in range(1, nb):
        other = lax.rem(mb + k, nb)
        norm_copy(mb, m.norm_batch, other, (other, me), "norm_batch", mb).start()
    while waiting:
        advance()
    for k in range(1, nb):
        other = lax.rem(mb + k, nb)
        norm_copy(mb, m.norm_batch, other, (other, me), "norm_batch", other).wait_recv()
    total = m.norm_batch[0]
    for k in range(1, nb):
        total = total + m.norm_batch[k]
    norm_out[...] = total

    for k in range(1, nw):
        other = lax.rem(me + k, nw)
        norm_copy(me, m.norm_all, other, (mb, other), "norm_all", me).wait_send()
    for k in range(1, nb):
        other = lax.rem(mb + k, nb)
        norm_copy(mb, m.norm_batch, other, (other, me), "norm_batch", mb).wait_send()
    for s in range(ns):
        gather_end(*ins, s)
        gather_end(*cots, s)
        scatter_end(*outs, 2, s)
        scatter_end(*gis, 3, s)


def per_device(nb, nw, inputs, lengths, gain1, bias1, w_qkv, w_out, gain2, bias2, w_up, w_down, cotangent):
    count, block, width = inputs.shape
    layers, _, hidden = w_up.shape
    ns, per = count // nw, block // WINDOW
    pieces = plan(nb, nw, ns, nw * per, width, hidden, layers)
    shape = (nw, ns, per, WINDOW, width)
    anywhere = pl.BlockSpec(memory_space=pl.ANY)
    vmem = pl.BlockSpec(memory_space=pltpu.VMEM)
    rows = 12 * CHUNK

    def body(*refs):
        kernel(nb, nw, ns, list(pieces), *refs)

    outputs, grad_rows, grads, norms = pl.pallas_call(
        body,
        out_shape=(
            jax.ShapeDtypeStruct(shape, BF16),
            jax.ShapeDtypeStruct(shape, BF16),
            jax.ShapeDtypeStruct((layers, rows, CHUNK), BF16),
            jax.ShapeDtypeStruct((4 * layers, width), F32),
        ),
        in_specs=[pl.BlockSpec(memory_space=pltpu.SMEM)] + [anywhere] * 2 + [vmem] * 4 + [anywhere] * 4,
        out_specs=(anywhere, anywhere, anywhere, vmem),
        scratch_shapes=list(pieces.values()),
        compiler_params=pltpu.CompilerParams(
            collective_id=0, has_side_effects=True, vmem_limit_bytes=64 * 1024 * 1024
        ),
    )(
        lengths, inputs.reshape(shape), cotangent.reshape(shape),
        gain1, bias1, gain2, bias2, w_qkv, w_out, w_up, w_down,
    )
    each = hidden // CHUNK
    tokens = count * block // layers

    def finish(out_in, rows_in, grads_in, norm_in, *results):
        out_out, rows_out, qkv_out, rest_out, up_out, down_out, *norm_outs = results
        out_out[...] = out_in[...]
        rows_out[...] = rows_in[...].astype(F32)

        def part(c):
            return grads_in[0, c * CHUNK : (c + 1) * CHUNK].astype(F32)

        for c in range(each):
            up_out[0, :, c * CHUNK : (c + 1) * CHUNK] = part(c)
            down_out[0, c * CHUNK : (c + 1) * CHUNK] = part(each + c)
        rest_out[0] = part(2 * each)
        for c in range(3):
            qkv_out[0, :, c * CHUNK : (c + 1) * CHUNK] = part(2 * each + 1 + c)
        for l in range(layers):
            for k in range(4):
                norm_outs[k][l : l + 1] = norm_in[4 * l + k : 4 * l + k + 1]

    row_spec = pl.BlockSpec((tokens, width), lambda i: (i, 0))
    norm_spec = pl.BlockSpec((layers, width), lambda i: (0, 0))

    def layer_spec(*dims):
        return pl.BlockSpec((1, *dims), lambda i: (i, 0, 0))

    outputs, grad_rows, grad_qkv, grad_out, grad_up, grad_down, *norms = pl.pallas_call(
        finish,
        grid=(layers,),
        out_shape=(
            jax.ShapeDtypeStruct((count * block, width), BF16),
            jax.ShapeDtypeStruct((count * block, width), F32),
            jax.ShapeDtypeStruct((layers, width, 3 * width), F32),
            jax.ShapeDtypeStruct((layers, width, width), F32),
            jax.ShapeDtypeStruct((layers, width, hidden), F32),
            jax.ShapeDtypeStruct((layers, hidden, width), F32),
        )
        + (jax.ShapeDtypeStruct((layers, width), F32),) * 4,
        in_specs=[
            row_spec,
            row_spec,
            layer_spec(rows, CHUNK),
            pl.BlockSpec((4 * layers, width), lambda i: (0, 0)),
        ],
        out_specs=(
            row_spec,
            row_spec,
            layer_spec(width, 3 * width),
            layer_spec(width, width),
            layer_spec(width, hidden),
            layer_spec(hidden, width),
        )
        + (norm_spec,) * 4,
        compiler_params=pltpu.CompilerParams(vmem_limit_bytes=60 * 1024 * 1024),
    )(outputs.reshape(count * block, width), grad_rows.reshape(count * block, width), grads, norms)
    return (
        outputs.reshape(count, block, width),
        grad_rows.reshape(count, block, width),
        norms[0],
        norms[1],
        grad_qkv,
        grad_out,
        norms[2],
        norms[3],
        grad_up,
        grad_down,
    )


def solution(mesh):
    nb, nw = mesh.shape["batch"], mesh.shape["wide"]

    def step(*args):
        return per_device(nb, nw, *args)

    rows = P("batch", "wide", None)
    return jax.shard_map(
        step,
        mesh=mesh,
        in_specs=(rows, P("batch")) + (P(),) * 8 + (rows,),
        out_specs=(rows, rows) + (P(),) * 8,
        check_vma=False,
    )
```

time: 829 us -> 141 us (0.17); the launches traced: 819 us -> 141 us
  waiting for transfers between devices: 367 us -> 0 us
  local copies, waits for them, and re-layouts: 183 us -> 0 us
  Pallas kernels: 0 us -> 140 us
  matrix products: 109 us -> 0 us
  other arithmetic: 83.6 us -> 0 us
  blocking collectives: 41 us -> 0 us
  starting transfers between devices: 19 us -> 0 us
  between operations: 16.1 us -> 0.83 us
    pallas_call x0 -> x2, Pallas kernels: none -> 140 us  [the longest x1 135 us: per_device(): pl.pallas_call(body, out_shape=(jax.ShapeDtypeStruct(shape, BF16), jax.Sh...]
    dot_general x42 -> x0, matrix products: 109 us -> none  [the longest x4 17.8 us: attend_forward(): jnp.einsum(einsum_forms[1], weights, value_part, preferred_element_type=j...]
    unnamed x304 -> x0, local copies, waits for them, and re-layouts: 105 us -> none
    psum x1 -> x0, waiting for transfers between devices: 99.4 us -> none  [per_device(): summed = lax.psum(stacked, ('batch', 'wide'))]
    ppermute x4 -> x0, waiting for transfers between devices: 97.8 us -> none  [shifted(): return lax.ppermute(block, axis, route)]
    all_gather x2 -> x0, waiting for transfers between devices: 92.3 us -> none  [layer_forward(): far_all = lax.all_gather(far_own, 'wide', axis=1, tiled=True)]
    unnamed x7 -> x0, waiting for transfers between devices: 77.4 us -> none
    psum x1 -> x0, blocking collectives: 41 us -> none  [per_device(): summed = lax.psum(stacked, ('batch', 'wide'))]
  transfers between devices with their start and end apart: 9 -> 0, of which waited for: 9 -> 0; matrix products, arithmetic and copies ran while one was open for 11% -> 0% of each run, Pallas kernels for 0% -> 0%
where the time goes in v1:
time: 141 us
  Pallas kernels  140 us (99%)
    pallas_call x1, Pallas kernels, per_device(): pl.pallas_call(body, out_shape=(jax.ShapeDtypeStruct(shape, BF16), jax.Sh...  135 us
    pallas_call x1, Pallas kernels, per_device(): pl.pallas_call(finish, grid=(layers,), out_shape=(jax.ShapeDtypeStruct((c...  5.71 us

profile of v1, /device:TPU:1, one launch (start us, length us, event | category | flops | bytes accessed | tf_op | source)
XLA Modules:
  0.0 141.2 jit_solution(1170494499733270160)
XLA Ops:
  0.6 134.7 %shard_map.186 = (bf16[8,2,1,128,256]{4,3,2,1,0:T(8,128)(2,1)}, bf16[8,2,1,128,256]{4,3,2,1,0:T(8,128)(2,1)}, bf16[2,3072,256]{2,1,0:T(8,128)(2,1)}, f32[8,256]{1,0:T(8,128)}) custom-call(s32[16]{0:T(128)} %refs_0_.1, bf16[8,2,1,128,256]{4,3,2,1,0:T(8,128)(2,1)} %bitcast.8, bf16[8,2,1,128,256]{4,3,2,1,0:T(8,128)(2,1)} %bitcast.9, f32[2,256]{1,0:T(2,128)} %refs_3_.1, ...), custom_call_target="tpu_custom_call" | custom-call | tf_op jit(solution)/shard_map/pallas_call | solution.py:808
  135.3 5.7 %shard_map.187 = (bf16[2048,256]{1,0:T(8,128)(2,1)}, f32[2048,256]{1,0:T(8,128)}, f32[2,256,768]{2,1,0:T(8,128)}, f32[2,256,256]{2,1,0:T(8,128)}, f32[2,256,1024...) custom-call(bf16[2048,256]{1,0:T(8,128)(2,1)} %bitcast.6, ...), custom_call_target="tpu_custom_call" | custom-call | tf_op jit(solution)/shard_map/pallas_call | solution.py:853

commit v2 on v1

--- a/solution.py
+++ b/solution.py
@@ -136,8 +136,8 @@
     vmem("got_pair", (layers, rows // 4 // nb, CHUNK), BF16)
     top = max(nw.bit_length() - 3, 1)
     vmem("got_top", (layers, top, rows // 4 // nb, CHUNK), BF16)
-    vmem("put_core", (hidden, CHUNK), BF16)
-    vmem("put_batch", (hidden, CHUNK), BF16)
+    vmem("put_core", (hidden + CHUNK // 2, CHUNK), BF16)
+    vmem("put_batch", (hidden + CHUNK // 2, CHUNK), BF16)
     vmem("put_pair", (rows // 4 // nb, CHUNK), BF16)
     vmem("put_top", (top, rows // 4 // nb, CHUNK), BF16)
     vmem("norm_all", (nw, 4 * layers, width), F32)
@@ -213,11 +213,12 @@
             gather_copy(src, dst, send, recv, s, partner(k), me).start()
         gather_own(src, dst, which, s).start()
 
-    def gather_wait(src, dst, send, recv, which, s):
-        for k in range(1, nw):
+    def gather_wait(src, dst, send, recv, which, s, steps=None):
+        for k in range(1, nw) if steps is None else steps:
             other = partner(k)
             gather_copy(src, dst, send, recv, s, other, other).wait_recv()
-        gather_own(src, dst, which, s).wait()
+        if steps is None or steps is close:
+            gather_own(src, dst, which, s).wait()
 
     def gather_end(src, dst, send, recv, s):
         for k in range(1, nw):
@@ -238,10 +239,11 @@
             src.at[pl.ds(s * nblk + me * per, per)], dst.at[me, s], m.own.at[which, s]
         )
 
-    def scatter_start(src, dst, send, recv, which, s):
-        for k in turns:
+    def scatter_start(src, dst, send, recv, which, s, steps=None):
+        for k in turns if steps is None else steps:
             scatter_copy(src, dst, send, recv, s, partner(k), me).start()
-        scatter_own(src, dst, which, s).start()
+        if steps is None or steps is close:
+            scatter_own(src, dst, which, s).start()
 
     def scatter_end(src, dst, send, recv, which, s):
         for k in range(1, nw):
@@ -542,11 +544,10 @@
     def grads_feed(l, s):
         outer(l, s, (m.a2_t if roomy else m.a2).at[l], m.slope.at[l], 0)
         outer(l, s, m.df_t, m.act.at[l], hidden // CHUNK, True)
+        outer(l, s, m.heads_t, m.dm, 2 * hidden // CHUNK)
 
     def grads_attend(l, s):
-        first = 2 * hidden // CHUNK
-        outer(l, s, m.heads_t, m.dm, first)
-        outer(l, s, (m.a1_t if roomy else m.a1).at[l], m.qkv.at[l], first + 1)
+        outer(l, s, (m.a1_t if roomy else m.a1).at[l], m.qkv.at[l], 2 * hidden // CHUNK + 1)
 
     core = lax.rem(me, 2)
     second = lax.rem(me // 2, 2)
@@ -556,8 +557,10 @@
         size = 2**bit
         return me + size - 2 * size * lax.rem(me // size, 2)
 
+    split = 2 * hidden + (CHUNK if CHUNK % (64 * nb) == 0 else 0)
+
     def reduction(l, which):
-        start, count = ((0, 2 * hidden), (2 * hidden, 4 * CHUNK))[which]
+        start, count = ((0, split), (split, 12 * CHUNK - split))[which]
         half, chunk, piece = count // 2, count // 2 // nb, count // 4 // nb
         lead = start // 2
         final = m.final.at[l]
@@ -708,9 +711,11 @@
 
     for s in range(ns):
         last = s == ns - 1
-        gather_wait(*ins, 0, s)
+        gather_wait(*ins, 0, s, close)
+        gather_wait(*ins, 0, s, far[: len(far) // 2])
         if s == 0:
             gather_start(*cots, 1, s)
+        gather_wait(*ins, 0, s, far[len(far) // 2 :])
         for l in range(layers):
             with jax.named_scope("layer_forward"):
                 forward(l, s)
@@ -742,7 +747,10 @@
                 back_project(l, s)
             if l == 0:
                 advance()
-        scatter_start(*gis, 3, s)
+        if not last:
+            scatter_start(*gis, 3, s)
+    scatter_start(*gis, 3, ns - 1, far[: len(far) // 2])
+    scatter_start(*gis, 3, ns - 1, close)
 
     def norm_copy(own, slots, k, device, name, owner):
         return pltpu.make_async_remote_copy(
@@ -758,7 +766,9 @@
     for k in range(1, nw):
         other = lax.rem(me + k, nw)
         norm_copy(me, m.norm_all, other, (mb, other), "norm_all", me).start()
-    advance()
+    for _ in range(3):
+        advance()
+    scatter_start(*gis, 3, ns - 1, far[len(far) // 2 :])
     for k in range(1, nw):
         other = lax.rem(me + k, nw)
         norm_copy(me, m.norm_all, other, (mb, other), "norm_all", other).wait_recv()

time: 141 us -> 138 us (0.979)
  Pallas kernels: 140 us -> 137 us
    pallas_call x1, Pallas kernels: 135 us -> 132 us  [per_device(): pl.pallas_call(body, out_shape=(jax.ShapeDtypeStruct(shape, BF16), jax.Sh...]
where the time goes in v2:
time: 138 us
  Pallas kernels  137 us (99%)
    pallas_call x1, Pallas kernels, per_device(): pl.pallas_call(body, out_shape=(jax.ShapeDtypeStruct(shape, BF16), jax.Sh...  132 us
    pallas_call x1, Pallas kernels, per_device(): pl.pallas_call(finish, grid=(layers,), out_shape=(jax.ShapeDtypeStruct((c...  5.71 us

profile of v2, /device:TPU:1, one launch (start us, length us, event | category | flops | bytes accessed | tf_op | source)
XLA Modules:
  0.0 138.3 jit_solution(11607824137689203848)
XLA Ops:
  0.6 131.7 %shard_map.186 = (bf16[8,2,1,128,256]{4,3,2,1,0:T(8,128)(2,1)}, bf16[8,2,1,128,256]{4,3,2,1,0:T(8,128)(2,1)}, bf16[2,3072,256]{2,1,0:T(8,128)(2,1)}, f32[8,256]{1,0:T(8,128)}) custom-call(s32[16]{0:T(128)} %refs_0_.1, bf16[8,2,1,128,256]{4,3,2,1,0:T(8,128)(2,1)} %bitcast.8, bf16[8,2,1,128,256]{4,3,2,1,0:T(8,128)(2,1)} %bitcast.9, f32[2,256]{1,0:T(2,128)} %refs_3_.1, ...), custom_call_target="tpu_custom_call" | custom-call | tf_op jit(solution)/shard_map/pallas_call | solution.py:818
  132.4 5.7 %shard_map.187 = (bf16[2048,256]{1,0:T(8,128)(2,1)}, f32[2048,256]{1,0:T(8,128)}, f32[2,256,768]{2,1,0:T(8,128)}, f32[2,256,256]{2,1,0:T(8,128)}, f32[2,256,1024...) custom-call(bf16[2048,256]{1,0:T(8,128)(2,1)} %bitcast.6, ...), custom_call_target="tpu_custom_call" | custom-call | tf_op jit(solution)/shard_map/pallas_call | solution.py:863

commit v3 on v2

--- a/solution.py
+++ b/solution.py
@@ -82,6 +82,10 @@
     g = h * q
     slope = q + g * (1.0 - q) * (6.0 * GELU_B * square + 2.0 * GELU_A)
     return g.astype(BF16), slope.astype(BF16)
+
+
+def first_rows(nb, hidden):
+    return 2 * hidden + (CHUNK if CHUNK % (64 * nb) == 0 else 0)
 
 
 def plan(nb, nw, ns, nblk, width, hidden, layers):
@@ -136,8 +140,8 @@
     vmem("got_pair", (layers, rows // 4 // nb, CHUNK), BF16)
     top = max(nw.bit_length() - 3, 1)
     vmem("got_top", (layers, top, rows // 4 // nb, CHUNK), BF16)
-    vmem("put_core", (hidden + CHUNK // 2, CHUNK), BF16)
-    vmem("put_batch", (hidden + CHUNK // 2, CHUNK), BF16)
+    vmem("put_core", (first_rows(nb, hidden) // 2, CHUNK), BF16)
+    vmem("put_batch", (rows // 2, CHUNK), BF16)
     vmem("put_pair", (rows // 4 // nb, CHUNK), BF16)
     vmem("put_top", (top, rows // 4 // nb, CHUNK), BF16)
     vmem("norm_all", (nw, 4 * layers, width), F32)
@@ -557,7 +561,7 @@
         size = 2**bit
         return me + size - 2 * size * lax.rem(me // size, 2)
 
-    split = 2 * hidden + (CHUNK if CHUNK % (64 * nb) == 0 else 0)
+    split = first_rows(nb, hidden)
 
     def reduction(l, which):
         start, count = ((0, split), (split, 12 * CHUNK - split))[which]
@@ -597,7 +601,7 @@
 
         def to_batch(other, owner):
             return remote(
-                m.put_batch.at[span(other * chunk, chunk)],
+                m.put_batch.at[span(lead + other * chunk, chunk)],
                 m.got_batch.at[l, owner, pl.ds(start // 2 // nb, chunk)],
                 "batch", other, owner, (other, me),
             )
@@ -630,7 +634,7 @@
             to_core.wait()
             total = m.grad[l, span(mine, half)] + m.got_core[l, pl.ds(lead, half)].astype(F32)
             m.grad[l, span(mine, half)] = total
-            m.put_batch[pl.ds(0, half)] = total.astype(BF16)
+            m.put_batch[pl.ds(lead, half)] = total.astype(BF16)
             for other in others():
                 to_batch(other, mb).start()
 
@@ -698,7 +702,7 @@
     waiting = []
 
     def advance():
-        for steps in list(waiting):
+        for steps in waiting[::-1]:
             steps.pop(0)()
             if not steps:
                 waiting.remove(steps)

time: 138 us -> 141 us (1.022)
  Pallas kernels: 137 us -> 140 us
    pallas_call x1, Pallas kernels: 132 us -> 135 us  [per_device(): pl.pallas_call(body, out_shape=(jax.ShapeDtypeStruct(shape, BF16), jax.Sh...]
where the time goes in v3:
time: 141 us
  Pallas kernels  140 us (99%)
    pallas_call x1, Pallas kernels, per_device(): pl.pallas_call(body, out_shape=(jax.ShapeDtypeStruct(shape, BF16), jax.Sh...  135 us
    pallas_call x1, Pallas kernels, per_device(): pl.pallas_call(finish, grid=(layers,), out_shape=(jax.ShapeDtypeStruct((c...  5.71 us

profile of v3, /device:TPU:1, one launch (start us, length us, event | category | flops | bytes accessed | tf_op | source)
XLA Modules:
  0.0 141.3 jit_solution(5641986099784313954)
XLA Ops:
  0.6 134.7 %shard_map.186 = (bf16[8,2,1,128,256]{4,3,2,1,0:T(8,128)(2,1)}, bf16[8,2,1,128,256]{4,3,2,1,0:T(8,128)(2,1)}, bf16[2,3072,256]{2,1,0:T(8,128)(2,1)}, f32[8,256]{1,0:T(8,128)}) custom-call(s32[16]{0:T(128)} %refs_0_.1, bf16[8,2,1,128,256]{4,3,2,1,0:T(8,128)(2,1)} %bitcast.8, bf16[8,2,1,128,256]{4,3,2,1,0:T(8,128)(2,1)} %bitcast.9, f32[2,256]{1,0:T(2,128)} %refs_3_.1, ...), custom_call_target="tpu_custom_call" | custom-call | tf_op jit(solution)/shard_map/pallas_call | solution.py:822
  135.4 5.7 %shard_map.187 = (bf16[2048,256]{1,0:T(8,128)(2,1)}, f32[2048,256]{1,0:T(8,128)}, f32[2,256,768]{2,1,0:T(8,128)}, f32[2,256,256]{2,1,0:T(8,128)}, f32[2,256,1024...) custom-call(bf16[2048,256]{1,0:T(8,128)(2,1)} %bitcast.6, ...), custom_call_target="tpu_custom_call" | custom-call | tf_op jit(solution)/shard_map/pallas_call | solution.py:867

commit v4 on v2

--- a/solution.py
+++ b/solution.py
@@ -371,13 +371,12 @@
     def forward(l, s):
         length = lens[me * ns + s]
 
-        def project(t):
-            for b, r, _ in parts_of(rows_of(t)):
+        def project(rows, lanes):
+            for b, r, _ in parts_of(rows):
                 store_norm(l, 0, b, r, source(l, s, b, r), m.a1, gain1, bias1)
-            rows = rows_of(t)
             a = flat(m.a1[l, rows])
             if roomy:
-                m.a1_t[l, :, lanes_of(t)] = a.T
+                m.a1_t[l, :, lanes] = a.T
             m.qkv[l, rows] = blocks(dot(a, m.w_qkv[l]).astype(BF16))
 
         here = m.qkv.at[l]
@@ -421,7 +420,10 @@
                 else:
                     m.dx[b, r] = y
 
-        loop(tiles, project)
+        if roomy:
+            project(pl.ds(0, nblk), pl.ds(0, nblk * WINDOW))
+        else:
+            loop(tiles, lambda t: project(rows_of(t), lanes_of(t)))
         loop(groups // AT_ONCE, attend)
         loop(tiles, mix)
 
@@ -514,11 +516,11 @@
             here[b, :, Q_NEAR] = m.near_dq[b]
 
     def back_project(l, s):
-        def body(t):
-            da = back_dot(flat(m.qkv[l, rows_of(t)]), "w_qkv", l)
+        def body(rows):
+            da = back_dot(flat(m.qkv[l, rows]), "w_qkv", l)
             over = 1.0 / gain1[l : l + 1]
             terms = []
-            for b, r, i in parts_of(rows_of(t)):
+            for b, r, i in parts_of(rows):
                 back, *term = unnorm(l, 0, b, r, da[i], m.a1, gain1, bias1, over)
                 terms.append(term)
                 if l == 0:
@@ -527,7 +529,10 @@
                     m.dx[b, r] = m.dx[b, r] + back
             add_sums(l, 0, terms)
 
-        loop(tiles, body)
+        if roomy:
+            body(pl.ds(0, nblk))
+        else:
+            loop(tiles, lambda t: body(rows_of(t)))
 
     def outer(l, s, left, ref, first, flipped=False):
         if len(left.shape) == 2:

time: 138 us -> 139 us (level)
  no operation moved by 1% of the time
where the time goes in v4:
time: 139 us
  Pallas kernels  138 us (99%)
    pallas_call x1, Pallas kernels, per_device(): pl.pallas_call(body, out_shape=(jax.ShapeDtypeStruct(shape, BF16), jax.Sh...  132 us
    pallas_call x1, Pallas kernels, per_device(): pl.pallas_call(finish, grid=(layers,), out_shape=(jax.ShapeDtypeStruct((c...  5.71 us

profile of v4, /device:TPU:1, one launch (start us, length us, event | category | flops | bytes accessed | tf_op | source)
XLA Modules:
  0.0 138.7 jit_solution(5482928293442953143)
XLA Ops:
  0.6 132.2 %shard_map.186 = (bf16[8,2,1,128,256]{4,3,2,1,0:T(8,128)(2,1)}, bf16[8,2,1,128,256]{4,3,2,1,0:T(8,128)(2,1)}, bf16[2,3072,256]{2,1,0:T(8,128)(2,1)}, f32[8,256]{1,0:T(8,128)}) custom-call(s32[16]{0:T(128)} %refs_0_.1, bf16[8,2,1,128,256]{4,3,2,1,0:T(8,128)(2,1)} %bitcast.8, bf16[8,2,1,128,256]{4,3,2,1,0:T(8,128)(2,1)} %bitcast.9, f32[2,256]{1,0:T(2,128)} %refs_3_.1, ...), custom_call_target="tpu_custom_call" | custom-call | tf_op jit(solution)/shard_map/pallas_call | solution.py:823
  132.8 5.7 %shard_map.187 = (bf16[2048,256]{1,0:T(8,128)(2,1)}, f32[2048,256]{1,0:T(8,128)}, f32[2,256,768]{2,1,0:T(8,128)}, f32[2,256,256]{2,1,0:T(8,128)}, f32[2,256,1024...) custom-call(bf16[2048,256]{1,0:T(8,128)(2,1)} %bitcast.6, ...), custom_call_target="tpu_custom_call" | custom-call | tf_op jit(solution)/shard_map/pallas_call | solution.py:868
